TPU v7x, 128 devices: a whole 4x4x4 slice. The times are simulated.
128 devices in a mesh: win: 4 (over x), chan: 32 (over y, z, core).
Axes of the slice: x: 4, y: 4, z: 4, core: 2. Of those that a mesh axis runs over, the one named last changes fastest.
Arguments:
- traces: bfloat16 [2048, 16, 14976], P('chan', 'win'), may hold values from -100 to 100
- fetch_rows: int32 [32, 32, 8], replicated, may hold values from 0 to 63, as said below
- pair_slots: int32 [512, 2, 128], P('chan'), may hold values from 0 to 255, as said below
- tile_count: int32 [32], P('chan'), may hold values from 1 to 16, 256 in all
Outputs:
- stacks: float32 [512, 128, 2001], P('chan', 'win')
Inputs may be any that keep to these rules, and one draw needn't show every extreme that they name: `fetch_rows`: the 8 entries of one owner and one block are distinct channels of that block. `pair_slots`: the source and receiver entries of a pair differ. `tile_count`: the counts of all owners add up to 256.
All inputs are finite; a program needn't handle non-finite values. No bound on the sum of `tile_count` on one device may be relied on, other than what follows from the above.
Results may differ from a plain program's by a relative error of at most 0.0094.
Values may be sent and summed in bfloat16 or wider, within the bound.
A program may use at most 128 MiB of HBM per device.

v0:
```python
import math

import jax
import jax.numpy as jnp
from jax import lax
from jax.sharding import PartitionSpec as P

FREQS = 512
SMOOTH = 64
LOW_BIN = 60
MAXLAG = 1000


def band_table(length, first_bin, band_bins):
    samples = lax.broadcasted_iota(jnp.int32, (length, band_bins), 0)
    bin_index = lax.broadcasted_iota(jnp.int32, (length, band_bins), 1) + first_bin
    phase_index = samples * bin_index % length
    angles = phase_index.astype(jnp.float32) * (2.0 * math.pi / length)
    return jnp.concatenate([jnp.cos(angles), -jnp.sin(angles)], axis=1)


def lag_table(length, first_bin, band_bins, max_lag, lag_scale):
    lag_count = 2 * max_lag + 1
    bin_index = lax.broadcasted_iota(jnp.int32, (band_bins, lag_count), 0) + first_bin
    lag_index = lax.broadcasted_iota(jnp.int32, (band_bins, lag_count), 1) - max_lag + length
    phase_index = bin_index * lag_index % length
    angles = phase_index.astype(jnp.float32) * (2.0 * math.pi / length)
    return jnp.concatenate([jnp.cos(angles) * lag_scale, -jnp.sin(angles) * lag_scale], axis=0)


def whiten(spectra, band_bins, smooth_bins):
    real_part = spectra[:, :band_bins]
    imag_part = spectra[:, band_bins:]
    magnitude = jnp.sqrt(real_part * real_part + imag_part * imag_part)
    level_mean = jnp.mean(
        magnitude.reshape(magnitude.shape[0], band_bins // smooth_bins, smooth_bins), axis=2
    )
    level_full = jnp.repeat(level_mean, smooth_bins, axis=1) + 1e-06
    return jnp.concatenate([real_part / level_full, imag_part / level_full], axis=1).astype(
        jnp.bfloat16
    )


def cross_spectra(channel_table, tile_slots, band_bins):
    source_rows = jnp.take(channel_table, tile_slots[:, 0, :], axis=0).astype(jnp.float32)
    receiver_rows = jnp.take(channel_table, tile_slots[:, 1, :], axis=0).astype(jnp.float32)
    source_re = source_rows[..., :band_bins]
    source_im = source_rows[..., band_bins:]
    receiver_re = receiver_rows[..., :band_bins]
    receiver_im = receiver_rows[..., band_bins:]
    real_part = jnp.sum(source_re * receiver_re + source_im * receiver_im, axis=2)
    imag_part = jnp.sum(source_im * receiver_re - source_re * receiver_im, axis=2)
    return jnp.concatenate([real_part, imag_part], axis=-1)


def body(traces, fetch_rows, pair_slots, tile_count):
    chan_rows, win_local, length = traces.shape
    row_width = win_local * 2 * FREQS
    dft_table = band_table(length, LOW_BIN, FREQS).astype(jnp.bfloat16)
    spectra = jnp.dot(
        traces.reshape(chan_rows * win_local, length), dft_table, preferred_element_type=jnp.float32
    )
    whitened = whiten(spectra, FREQS, SMOOTH).reshape(chan_rows, row_width)
    chan_count = lax.axis_size("chan")
    my_index = lax.axis_index("chan")
    every_row = lax.all_gather(whitened, "chan", axis=0, tiled=True)
    my_lists = lax.dynamic_index_in_dim(fetch_rows, my_index, 0, keepdims=False)
    offsets = jnp.arange(chan_count, dtype=jnp.int32)[:, None] * chan_rows
    channel_table = jnp.take(every_row, (my_lists + offsets).reshape(-1), axis=0)
    channel_table = channel_table.reshape(-1, win_local, 2 * FREQS)
    slot_count, _, pair_width = pair_slots.shape
    live_count = tile_count[0]

    def add_tile(tile_pos, cross_all):
        tile_slots = lax.dynamic_slice_in_dim(pair_slots, tile_pos, 1, 0)
        return lax.dynamic_update_slice_in_dim(
            cross_all, cross_spectra(channel_table, tile_slots, FREQS), tile_pos, 0
        )

    cross_all = lax.fori_loop(
        0, live_count, add_tile, jnp.zeros((slot_count, pair_width, 2 * FREQS), jnp.float32)
    )
    windows_all = win_local * lax.axis_size("win")
    inverse = lag_table(length, LOW_BIN, FREQS, MAXLAG, 1.0 / math.sqrt(FREQS * windows_all))
    summed = lax.psum_scatter(cross_all, "win", scatter_dimension=1, tiled=True)
    share_width = summed.shape[1]
    lagged = jnp.dot(
        summed.reshape(slot_count * share_width, 2 * FREQS),
        inverse,
        precision=lax.Precision.HIGHEST,
        preferred_element_type=jnp.float32,
    )
    return lagged.reshape(slot_count, share_width, -1)


def solution(mesh):
    return jax.shard_map(
        body,
        mesh=mesh,
        in_specs=(P("chan", "win", None), P(), P("chan", None, None), P("chan")),
        out_specs=P("chan", "win", None),
        check_vma=False,
    )
```

profile of v0, /device:TPU:1, one launch (start us, length us, event | category | flops | bytes accessed | tf_op | source)
XLA Modules:
  0.0 544.5 jit_solution(13830665827744827612)
XLA Ops:
  6.5 131.5 %cosine_convert_fusion = (bf16[14976,512]{1,0:T(8,128)(2,1)}, bf16[14976,512]{1,0:T(8,128)(2,1)}) fusion(s32[512]{0:T(512)S(1)} %iota_add_fusion.1), kind=kLoop, calls=%fused_computation.27 | loop fusion | flops 92012544 | bytes 30672896 | tf_op jit(solution)/shard_map/convert.2
  138.0 11.4 %reshape.83 = bf16[256,14976]{1,0:T(8,128)(2,1)} reshape(bf16[64,4,14976]{2,1,0:T(4,128)(2,1)} %param.8) | data formatting | bytes 15335424 | tf_op jit(solution)/shard_map/reshape | solution.py:61
  149.5 15.4 %fusion.21 = f32[256,1024]{0,1:T(8,128)S(1)} fusion(bf16[256,14976]{1,0:T(8,128)(2,1)} %reshape.83, bf16[14976,512]{1,0:T(8,128)(2,1)} %get-tuple-element.58, bf16[14976,512]{1,0:T(8,128)(2,1)} %get-tuple-element.57), kind=kOutput, calls=%fused_computation.46 | convolution fusion | flops 7913078784 | bytes 39387136 | tf_op jit(solution)/shard_map/dot_general | solution.py:60
  167.4 75.6 %all-gather.2.cloned.1.call-done = bf16[2048,4096]{1,0:T(8,128)(2,1)} async-done(((bf16[64,4096]{1,0:T(8,128)(2,1)}), bf16[2048,4096]{1,0:T(8,128)(2,1)}) %all-gather.2.cloned.1.call-update) | async-done | bytes 16777232 | tf_op jit(solution)/shard_map/all_gather | solution.py:66
  243.0 11.8 %gather_fusion.2 = bf16[256,4096]{1,0:T(8,128)(2,1)S(1)} fusion(bf16[2048,4096]{1,0:T(8,128)(2,1)} %all-gather.2.cloned.1.call-done, s32[1024]{0:T(1024)S(1)} %pad_clamp_fusion.2), kind=kCustom, calls=%fused_computation.2 | custom fusion | bytes 4195328 | tf_op jit(solution)/shard_map/jit(_take)/gather | solution.py:69
  254.8 2.8 gather.10
  257.6 3.6 broadcast_select_fusion
  261.2 4.3 broadcast_in_dim.26
  265.5 98.7 %while.10 = (s32[]{:T(128)}, f32[16,128,1024]{2,1,0:T(8,128)}, s32[]{:T(128)}, s32[16,2,128]{2,1,0:T(2,128)}, bf16[256,4,1024]{2,1,0:T(4,128)(2,1)}, /*index=5*/s32[]{:T(128)}, s32[]{:T(128)}, s32[]{:T(128)}) while((s32[]{:T(128)}, f32[16,128,1024]{2,1,0:T(8,128)}, s32[]{:T(128)}, s32[16,2,128]{2,1,0:T(2,128)}, ...), condition=%wide.region_4.6_spmd, body=%wide.region_1.5_spmd.sunk | while | flops 4198661 | bytes 16268927 | solution.py:80
  267.1 3.0 gather_fusion.1
  270.6 3.0 gather_fusion
  277.9 3.0 gather_fusion.1
  281.5 3.0 gather_fusion
  285.0 1.6 add_reduce_fusion.2
  288.8 3.0 gather_fusion.1
  292.4 3.0 gather_fusion
  295.9 1.6 add_reduce_fusion.2
  299.7 3.0 gather_fusion.1
  303.2 3.0 gather_fusion
  310.5 3.0 gather_fusion.1
  314.1 3.0 gather_fusion
  321.4 3.0 gather_fusion.1
  325.0 3.0 gather_fusion
  332.3 3.0 gather_fusion.1
  335.8 3.0 gather_fusion
  343.1 3.0 gather_fusion.1
  346.7 3.0 gather_fusion
  354.0 3.0 gather_fusion.1
  357.6 3.0 gather_fusion
  364.2 19.5 %cosine_multiply_fusion = (f32[512,2001]{0,1:T(8,128)}, f32[512,2001]{0,1:T(8,128)}) fusion(s32[2001]{0:T(1024)S(1)} %iota_add_fusion, s32[512]{0:T(512)S(1)} %iota_add_fusion.1), kind=kLoop, calls=%fused_computation.40 | loop fusion | flops 12294144 | bytes 8206148 | tf_op jit(solution)/shard_map/mul | solution.py:28
  383.8 136.2 %reduce-scatter.2.cloned.1.call-done = f32[16,32,1024]{2,1,0:T(8,128)} async-done(((f32[16,128,1024]{2,1,0:T(8,128)}), f32[16,32,1024]{2,1,0:T(8,128)}) %reduce-scatter.2.cloned.1.call-update) | async-done | bytes 2097168 | tf_op jit(solution)/shard_map/reduce_scatter | solution.py:85
  520.0 17.7 %fusion.13 = f32[16,32,2001]{2,1,0:T(8,128)} fusion(f32[16,32,1024]{2,1,0:T(8,128)} %reduce-scatter.2.cloned.1.call-done, f32[512,2001]{0,1:T(8,128)} %get-tuple-element.56, f32[512,2001]{0,1:T(8,128)} %get-tuple-element.55), kind=kOutput, calls=%fused_computation.33 | convolution fusion | flops 12591252480 | bytes 14391296 | tf_op jit(solution)/shard_map/dot_general | solution.py:87
  (97 shorter events, 36.1 us)
Async XLA Ops:
  6.5 160.3 %copy-start = (s32[32,32,8]{1,2,0:T(8,128)S(1)}, s32[32,32,8]{1,2,0:T(8,128)}, u32[]{:S(2)}) copy-start(s32[32,32,8]{1,2,0:T(8,128)} %param.9) | copy-start | bytes 98308
  6.5 236.5 %all-gather.2.cloned.1.call-start = ((), (), s32[]{:S(2)}) async-start(), calls=%async_computation.1 | async-start | bytes 17301504 | tf_op jit(solution)/shard_map/all_gather | solution.py:66
  166.6 353.4 %reduce-scatter.2.cloned.1.call-start = ((), (), s32[]{:S(2)}) async-start(), calls=%async_computation.2 | async-start | bytes 10485760 | tf_op jit(solution)/shard_map/reduce_scatter | solution.py:85
  364.2 173.5 %copy-start.1 = (s32[32,32,8]{1,2,0:T(8,128)S(1)}, s32[32,32,8]{1,2,0:T(8,128)}, u32[]{:S(2)}) copy-start(s32[32,32,8]{1,2,0:T(8,128)} %param.9) | copy-start | bytes 98308
Sparse Core Ops, SparseCore 0:
  166.7 76.2 all-gather.1
  364.3 155.5 reduce-scatter.1
where the time goes:
time: 546 us; the launch traced here: 545 us
  waiting for transfers between devices  212 us (39%)
  other arithmetic  186 us (34%)
  local copies, waits for them, and re-layouts  92.9 us (17%)
  matrix products  33.1 us (6%)
  between operations  13.5 us (2%)
  loops' own time  7.25 us (1%)
    reduce_scatter x1, waiting for transfers between devices, body(): summed = lax.psum_scatter(cross_all, 'win', scatter_dimension=1, tiled=True)  136 us
    another operation x2, other arithmetic  132 us
    all_gather x1, waiting for transfers between devices, body(): every_row = lax.all_gather(whitened, 'chan', axis=0, tiled=True)  75.6 us
    gather x9, local copies, waits for them, and re-layouts, cross_spectra(): jnp.take(channel_table, tile_slots[:, 1, :], axis=0).astype(jnp.float32)  27.3 us
    gather x9, local copies, waits for them, and re-layouts, cross_spectra(): jnp.take(channel_table, tile_slots[:, 0, :], axis=0).astype(jnp.float32)  27.3 us
    mul x1, other arithmetic, lag_table(): jnp.cos(angles) * lag_scale  19.5 us
    dot_general x1, matrix products, body(): jnp.dot(summed.reshape(slot_count * share_width, 2 * FREQS), inverse, pre...  17.7 us
    dot_general x1, matrix products, body(): jnp.dot(traces.reshape(chan_rows * win_local, length), dft_table, preferr...  15.4 us
  transfers between devices with their start and end apart: 2, of which 2 were waited for; matrix products, arithmetic and copies ran while one was open for 4% of the time, Pallas kernels for 0%

commit v1 on v0

v1 whole, which is shorter than its diff:
```python
import functools
import math

import jax
import jax.numpy as jnp
import ml_dtypes
import numpy as np
from jax import lax
from jax.experimental import pallas as pl
from jax.experimental.pallas import tpu as pltpu
from jax.sharding import PartitionSpec as P

MESH=pl.DeviceIdType.MESH
S=14976
def quarter_table():
    s=np.arange(3840)[:,None]; k=np.arange(512)[None]+60
    a=((s*k)%S)*(2*math.pi/S)
    c=np.cos(a).reshape(3840,8,1,64); d=-np.sin(a).reshape(3840,8,1,64)
    return np.concatenate([c,d],2).reshape(3840,1024).astype(ml_dtypes.bfloat16)
def turn_rows():
    lane=np.arange(1024)%128; k=(np.arange(1024)//128)*64+lane%64; im=lane>=64
    s=np.where(k%2==0,1.,-1.)
    al=np.array([1,0,-1,0.])[k%4]
    be=np.where(im,np.array([0,-1,0,1.])[k%4],np.array([0,1,0,-1.])[k%4])
    return np.stack([s,al,be]+[s*0]*5).astype(np.float32)
FIRST=(0,30,59,88); COUNT=(30,29,29,29); SHIFT=(0,96,64,32)
CUT=15
def k1(x_ref,t_ref,r_ref,o_ref,xs,ts,acc,xsem,tsem):
    tp=[(0,1920+96),(2016,3840-2016)]
    tc=[pltpu.make_async_copy(t_ref.at[pl.ds(a,n)],ts.at[pl.ds(a,n)],tsem.at[i]) for i,(a,n) in enumerate(tp)]
    def xpiece(q,i):
        a=128*(FIRST[q]+(CUT if i else 0)); n=128*(COUNT[q]-CUT if i else CUT)
        return a,n
    xc={}
    for i in range(2):
        for q in range(4):
            a,n=xpiece(q,i)
            xc[q,i]=pltpu.make_async_copy(x_ref.at[:,:,pl.ds(a,n)],xs.at[:,:,pl.ds(a,n)],xsem.at[q,i])
    tc[0].start(); xc[0,0].start(); xc[1,0].start(); xc[2,0].start(); xc[3,0].start()
    tc[1].start()
    for q in range(4): xc[q,1].start()
    for i in range(2):
        tc[i].wait()
        for q in range(4):
            xc[q,i].wait()
            a,n=xpiece(q,i)
            x=xs[:,:,a:a+n].reshape(256,n)
            r0=SHIFT[q]+(128*CUT if i else 0)
            for j in range(4):
                cs=slice(256*j,256*j+256)
                y=jnp.dot(x,ts[r0:r0+n,cs],preferred_element_type=jnp.float32)
                acc[q,:,cs]=y if i==0 else acc[q,:,cs]+y
    for b in range(8):
        cs=slice(128*b,128*b+128)
        s,al,be=r_ref[0:1,cs],r_ref[1:2,cs],r_ref[2:3,cs]
        g0,g1,g2,g3=(acc[q,:,cs] for q in range(4))
        z=g0+s*g2+al*(g1+g3)+be*pltpu.roll(g1-g3,64,1)
        sq=z*z
        mag=jnp.sqrt(sq+pltpu.roll(sq,64,1))
        lev=jnp.sum(mag,axis=1,keepdims=True)*(1/128)+1e-6
        o_ref[b]=(z/lev).astype(jnp.bfloat16)
def dft(x,tab,turn):
    return pl.pallas_call(k1,out_shape=jax.ShapeDtypeStruct((8,256,128),jnp.bfloat16),
      in_specs=[pl.BlockSpec(memory_space=pl.ANY),pl.BlockSpec(memory_space=pl.ANY),pl.BlockSpec(memory_space=pltpu.VMEM)],
      out_specs=pl.BlockSpec(memory_space=pltpu.VMEM),
      scratch_shapes=[pltpu.VMEM((64,4,14976),jnp.bfloat16),pltpu.VMEM((3840,1024),jnp.bfloat16),pltpu.VMEM((4,256,1024),jnp.float32),
        pltpu.SemaphoreType.DMA((4,2)),pltpu.SemaphoreType.DMA((2,))],
      compiler_params=pltpu.CompilerParams(vmem_limit_bytes=56<<20))(x,tab,turn)
G=32
def k3(slots,count,t_ref,o_ref,a1,a2,r1,r2,sr):
    lane=lax.broadcasted_iota(jnp.int32,(1,1,128),2)
    sign=jnp.where(lane<64,1.0,-1.0).astype(jnp.float32)
    low=lax.broadcasted_iota(jnp.int32,(G,128),1)<64
    ri=lax.broadcasted_iota(jnp.int32,(256,256),0); ci=lax.broadcasted_iota(jnp.int32,(256,256),1); cl=ci%128
    one=lambda m,v: jnp.where(m,v,0.0).astype(jnp.bfloat16)
    perm=jnp.concatenate([one(ri==ci+jnp.where(cl<64,64,-64),jnp.where(cl<64,1.0,-1.0)),one(ri==ci-jnp.where(cl<64,0,64),1.0),one(ri==ci+jnp.where(cl<64,64,0),1.0)],1)
    def prep(i,_):
        rows=pl.ds(i*16,16)
        x=jnp.concatenate([t_ref[0,rows].reshape(256,128),t_ref[1,rows].reshape(256,128)],1)
        y=jnp.dot(x,perm,preferred_element_type=jnp.float32)
        for h in range(2):
            a1[rows,h]=t_ref[h,rows].astype(a1.dtype)
            for m,ref in enumerate((a2,r1,r2)):
                ref[rows,h]=y[:,256*m+128*h:256*m+128*h+128].reshape(16,16,128).astype(ref.dtype)
        return 0
    lax.fori_loop(0,16,prep,0)
    def tile(t,_):
        @pl.when(t<count[0])
        def _live():
            def reduce(w):
                for h in range(2):
                    v=[sr[w,h,pl.ds(j,G,stride=8)] for j in range(8)]
                    x=((v[0]+v[1])+(v[2]+v[3]))+((v[4]+v[5])+(v[6]+v[7]))
                    o_ref[h,w,pl.ds(pl.multiple_of(t*32,32),32)]=x.astype(jnp.bfloat16)
            for w in range(4):
                for i in range(G):
                    s=slots[t*256+w*G+i]; r=slots[t*256+128+w*G+i]
                    for h in range(2):
                        q=a1[s,h]*r1[r,h]+a2[s,h]*r2[r,h]
                        sr[w,h,pl.ds(8*i,8)]=q[:8]+q[8:]
                if w: reduce(w-1)
            reduce(3)
        @pl.when(t>=count[0])
        def _dead():
            for h in range(2):
                for w in range(4):
                    o_ref[h,w,pl.ds(pl.multiple_of(t*32,32),32)]=jnp.zeros((32,128),jnp.bfloat16)
        return 0
    lax.fori_loop(0,16,tile,0)
def cross(slots,count,tab):
    return pl.pallas_call(k3,out_shape=jax.ShapeDtypeStruct((2,4,512,128),jnp.bfloat16),
      in_specs=[pl.BlockSpec(memory_space=pltpu.SMEM),pl.BlockSpec(memory_space=pltpu.SMEM),pl.BlockSpec(memory_space=pltpu.VMEM)],
      out_specs=pl.BlockSpec(memory_space=pltpu.VMEM),
      scratch_shapes=[pltpu.VMEM((256,2,16,128),jnp.float32),pltpu.VMEM((256,2,16,128),jnp.float32),pltpu.VMEM((256,2,16,128),jnp.float32),pltpu.VMEM((256,2,16,128),jnp.float32),pltpu.VMEM((4,2,G*8,128),jnp.float32)],
      compiler_params=pltpu.CompilerParams(vmem_limit_bytes=30<<20))(slots.reshape(-1),count,tab.reshape(2,256,16,128))

def lag_rows():
    k=np.arange(512)[:,None]+60; l=np.arange(2001)[None]-1000+S
    a=((k*l)%S)*(2*math.pi/S); s=1/math.sqrt(8192)
    t=np.stack([(np.cos(a)*s).reshape(8,64,2001),(-np.sin(a)*s).reshape(8,64,2001)],1)
    return t.reshape(1024,2001).astype(ml_dtypes.bfloat16)
def lag_kernel(x_ref,t_ref,o_ref):
    x=jnp.concatenate([x_ref[h,w] for h in range(2) for w in range(4)],1)
    o_ref[...]=jnp.dot(x,t_ref[...],preferred_element_type=jnp.float32)
def lag(x,tab):
    return pl.pallas_call(lag_kernel,out_shape=jax.ShapeDtypeStruct((512,2001),jnp.float32),grid=(4,),
      in_specs=[pl.BlockSpec((2,4,128,128),lambda i:(0,0,i,0)),pl.BlockSpec((1024,2001),lambda i:(0,0))],
      out_specs=pl.BlockSpec((128,2001),lambda i:(i,0)),
      compiler_params=pltpu.CompilerParams(vmem_limit_bytes=40<<20))(x,tab)

def place():
    w=lax.axis_index("win"); m=lax.axis_index("chan")
    return w,m//8,(m//2)%4,m%2
def greet(devs):
    bar=pltpu.get_barrier_semaphore()
    for d in devs: pl.semaphore_signal(bar,inc=1,device_id=d,device_id_type=MESH)
    pl.semaphore_wait(bar,len(devs))
def route(fr,wh,o_ref,xr,xf,ff,dd,gg,ra,rb,sx,rx,s1,r1,s2,r2,ls):
    w,y,z,c=place()
    dev=lambda p:(w,p[0]*8+p[1]*2+p[2])
    me=y*8+z*2+c
    peers=[((y+d)%4,z,(c+e)%2) for d in (1,2,3) for e in (0,1)]+[(y,(z+d)%4,(c+e)%2) for d in range(4) for e in range(2) if (d,e)!=(0,0)]
    greet([((w+d)%4,me) for d in (1,2,3)]+[dev(p) for p in peers])
    px={}
    for h in range(2):
        for i,d in enumerate((2,1,3)):
            t=(w+d)%4
            cp=pltpu.make_async_remote_copy(src_ref=wh.at[h,t],dst_ref=xr.at[h,w],send_sem=sx.at[h,i],recv_sem=rx.at[h,i],device_id=(t,me),device_id_type=MESH)
            cp.start(); px[h,i]=cp
    own=pltpu.make_async_copy(wh.at[:,w],xr.at[:,w],ls.at[10]); own.start(); own.wait()
    p1=[]
    for h in range(2):
        for i in range(3): px[h,i].wait()
        for s in range(4):
            xf[s]=xr[h,s].astype(jnp.float32)
        for s in range(4):
            for i in range(4):
                ff[pl.ds(4*s+i,64,stride=16)]=xf[s,pl.ds(i,64,stride=4)]
        dd[h]=ff[...].astype(jnp.bfloat16).reshape(64,16,128)
        def pick(o,_):
            for j in range(8):
                gg[h,o//8,(o//2)%4,o%2,pl.ds(16*j,16)]=dd[h,fr[o*8+j]]
            return 0
        lax.fori_loop(0,32,pick,0)
        row=[]
        for i,d in enumerate((2,1,3)):
            yy=(y+d)%4; zz=(z+d)%4
            if h==0: cp=pltpu.make_async_remote_copy(src_ref=gg.at[0,yy],dst_ref=ra.at[y],send_sem=s1.at[0,i],recv_sem=r1.at[0,i],device_id=dev((yy,z,c)),device_id_type=MESH)
            else: cp=pltpu.make_async_remote_copy(src_ref=gg.at[1,:,zz],dst_ref=rb.at[z],send_sem=s1.at[1,i],recv_sem=r1.at[1,i],device_id=dev((y,zz,c)),device_id_type=MESH)
            cp.start(); row.append(cp)
        p1.append(row)
    la=pltpu.make_async_copy(gg.at[0,y],ra.at[y],ls.at[0]); la.start()
    lb=pltpu.make_async_copy(gg.at[1,:,z],rb.at[z],ls.at[1]); lb.start()
    la.wait(); lb.wait()
    p2=[]
    def send2(k):
        d=(0,2,1,3)[k]
        ys=(y-d)%4; zs=(z-d)%4
        j=0
        for dz in (2,1,3,0):
            for dc in (1,0):
                zz=(z+dz)%4; yy=(y+dz)%4; cc=(c+dc)%2
                if (dz,dc)==(0,0):
                    l1=pltpu.make_async_copy(ra.at[ys,z,c],o_ref.at[0,ys,z,c],ls.at[2+2*k]); l1.start()
                    l2=pltpu.make_async_copy(rb.at[zs,y,c],o_ref.at[1,y,zs,c],ls.at[3+2*k]); l2.start()
                    p2.append((l1,l2)); continue
                ca=pltpu.make_async_remote_copy(src_ref=ra.at[ys,zz,cc],dst_ref=o_ref.at[0,ys,z,c],send_sem=s2.at[0,k,j],recv_sem=r2.at[0,k,j],device_id=dev((y,zz,cc)),device_id_type=MESH); ca.start()
                cb=pltpu.make_async_remote_copy(src_ref=rb.at[zs,yy,cc],dst_ref=o_ref.at[1,y,zs,c],send_sem=s2.at[1,k,j],recv_sem=r2.at[1,k,j],device_id=dev((yy,z,cc)),device_id_type=MESH); cb.start()
                p2.append((ca,cb)); j+=1
    send2(0)
    for i in range(3):
        p1[0][i].wait(); p1[1][i].wait(); send2(i+1)
    for a,b in p2: a.wait(); b.wait()
def exchange(fr,wh):
    B=jnp.bfloat16; D=pltpu.SemaphoreType.DMA
    return pl.pallas_call(route,out_shape=jax.ShapeDtypeStruct((2,4,4,2,128,128),B),
      in_specs=[pl.BlockSpec(memory_space=pltpu.SMEM),pl.BlockSpec(memory_space=pltpu.VMEM)],out_specs=pl.BlockSpec(memory_space=pltpu.VMEM),
      scratch_shapes=[pltpu.VMEM((2,4,256,128),B),pltpu.VMEM((4,256,128),jnp.float32),pltpu.VMEM((1024,128),jnp.float32),pltpu.VMEM((2,64,16,128),B),
        pltpu.VMEM((2,4,4,2,128,128),B),pltpu.VMEM((4,4,2,128,128),B),pltpu.VMEM((4,4,2,128,128),B),
        D((2,3)),D((2,3)),D((2,3)),D((2,3)),D((2,4,7)),D((2,4,7)),D((11,))],
      compiler_params=pltpu.CompilerParams(collective_id=1,has_side_effects=True,vmem_limit_bytes=40<<20))(fr,wh)
def swap(x_ref,o_ref,ss,rs,ls):
    w,y,z,c=place(); me=y*8+z*2+c
    greet([((w+d)%4,me) for d in (1,2,3)])
    cps=[]
    for i,d in enumerate((2,1,3)):
        t=(w+d)%4
        cp=pltpu.make_async_remote_copy(src_ref=x_ref.at[:,t],dst_ref=o_ref.at[:,w],send_sem=ss.at[i],recv_sem=rs.at[i],device_id=(t,me),device_id_type=MESH)
        cp.start(); cps.append(cp)
    own=pltpu.make_async_copy(x_ref.at[:,w],o_ref.at[:,w],ls); own.start(); own.wait()
    for cp in cps: cp.wait()
def hand_over(x):
    D=pltpu.SemaphoreType.DMA
    return pl.pallas_call(swap,out_shape=jax.ShapeDtypeStruct(x.shape,x.dtype),
      in_specs=[pl.BlockSpec(memory_space=pltpu.VMEM)],out_specs=pl.BlockSpec(memory_space=pltpu.VMEM),
      scratch_shapes=[D((3,)),D((3,)),D],
      compiler_params=pltpu.CompilerParams(collective_id=2,has_side_effects=True,vmem_limit_bytes=20<<20))(x)

def body(traces,fetch_rows,pair_slots,tile_count):
    wh=dft(traces,jnp.asarray(quarter_table()),jnp.asarray(turn_rows()))
    fr=lax.dynamic_index_in_dim(fetch_rows,lax.axis_index("chan"),1,keepdims=False).reshape(-1)
    tab=exchange(fr,wh.reshape(2,4,256,128))
    part=cross(pair_slots,tile_count,tab)
    full=hand_over(part)
    return lag(full,jnp.asarray(lag_rows())).reshape(16,32,2001)

def solution(mesh):
    return jax.shard_map(body,mesh=mesh,in_specs=(P("chan","win",None),P(),P("chan",None,None),P("chan")),
      out_specs=P("chan","win",None),check_vma=False)
```

time: 546 us -> 91.1 us (0.17)
  waiting for transfers between devices: 212 us -> 0 us
  other arithmetic: 186 us -> 0 us
  local copies, waits for them, and re-layouts: 92.9 us -> 2.21 us
  Pallas kernels: 0 us -> 86.6 us
  matrix products: 33.1 us -> 0 us
  between operations: 13.5 us -> 0.77 us
  loops' own time: 7.25 us -> 0 us
    reduce_scatter x1 -> x0, waiting for transfers between devices: 136 us -> none  [body(): summed = lax.psum_scatter(cross_all, 'win', scatter_dimension=1, tiled=True)]
    another operation x2 -> x0, other arithmetic: 132 us -> none
    pallas_call x0 -> x5, Pallas kernels: none -> 86.6 us  [the longest x1 43.7 us: exchange(): pl.pallas_call(route, out_shape=jax.ShapeDtypeStruct((2, 4, 4, 2, 128, 12...]
    all_gather x1 -> x0, waiting for transfers between devices: 75.6 us -> none  [body(): every_row = lax.all_gather(whitened, 'chan', axis=0, tiled=True)]
    gather x20 -> x0, local copies, waits for them, and re-layouts: 69.2 us -> none  [the longest x9 27.3 us: cross_spectra(): jnp.take(channel_table, tile_slots[:, 1, :], axis=0).astype(jnp.float32)]
    dot_general x2 -> x0, matrix products: 33.1 us -> none  [the longest x1 17.7 us: body(): jnp.dot(summed.reshape(slot_count * share_width, 2 * FREQS), inverse, pre...]
    mul x2 -> x0, other arithmetic: 19.5 us -> none  [the longest x1 19.5 us: lag_table(): jnp.cos(angles) * lag_scale]
    reduce_sum x10 -> x0, other arithmetic: 14.3 us -> none  [the longest x9 14.1 us: cross_spectra(): jnp.sum(source_re * receiver_re + source_im * receiver_im, axis=2)]
  transfers between devices with their start and end apart: 2 -> 0, of which waited for: 2 -> 0; matrix products, arithmetic and copies ran while one was open for 4% -> 0% of each run, Pallas kernels for 0% -> 0%
where the time goes in v1:
time: 91.1 us; the launch traced here: 89.5 us
  Pallas kernels  86.6 us (95%)
  local copies, waits for them, and re-layouts  2.21 us (2%)
    pallas_call x1, Pallas kernels, exchange(): pl.pallas_call(route, out_shape=jax.ShapeDtypeStruct((2, 4, 4, 2, 128, 12...  43.7 us
    pallas_call x1, Pallas kernels, dft(): pl.pallas_call(k1, out_shape=jax.ShapeDtypeStruct((8, 256, 128), jnp.bflo...  15.5 us
    pallas_call x1, Pallas kernels, cross(): pl.pallas_call(k3, out_shape=jax.ShapeDtypeStruct((2, 4, 512, 128), jnp.b...  13.6 us
    pallas_call x1, Pallas kernels, hand_over(): pl.pallas_call(swap, out_shape=jax.ShapeDtypeStruct(x.shape, x.dtype), in...  9.48 us
    pallas_call x1, Pallas kernels, lag(): pl.pallas_call(lag_kernel, out_shape=jax.ShapeDtypeStruct((512, 2001), jn...  4.3 us

profile of v1, /device:TPU:1, one launch (start us, length us, event | category | flops | bytes accessed | tf_op | source)
XLA Modules:
  0.0 89.5 jit_solution(2420413659105523937)
XLA Ops:
  0.0 0.0 copy-start
  0.7 0.2 copy-done
  0.9 0.7 dynamic-slice_reduce_fusion
  1.6 0.1 reshape.17.fr
  1.7 0.0 copy-start.3
  1.7 15.5 %shard_map.73 = bf16[8,256,128]{2,1,0:T(8,128)(2,1)} custom-call(bf16[64,4,14976]{2,1,0:T(4,128)(2,1)} %x_ref.1, bf16[3840,1024]{1,0:T(8,128)(2,1)} %constant.16.clone.t_ref, f32[8,1024]{1,0:T(8,128)} %constant.17.clone.r_ref), custom_call_target="tpu_custom_call" | custom-call | tf_op jit(solution)/shard_map/pallas_call | solution.py:63
  17.2 0.0 copy-start.1
  17.2 0.0 copy-start.2
  17.3 1.2 %copy-done.2 = bf16[8,256,128]{2,1,0:T(8,128)(2,1)S(1)} copy-done((bf16[8,256,128]{2,1,0:T(8,128)(2,1)S(1)}, bf16[8,256,128]{2,1,0:T(8,128)(2,1)}, u32[]{:S(2)}) %copy-start.2) | copy-done | bytes 524312
  18.4 43.7 %shard_map.74 = bf16[2,4,4,2,128,128]{5,4,3,2,1,0:T(8,128)(2,1)S(1)} custom-call(s32[256]{0:T(256)S(1)} %reshape.17.fr, bf16[2,4,256,128]{3,2,1,0:T(8,128)(2,1)S(1)} %bitcast.5), custom_call_target="tpu_custom_call" | custom-call | tf_op jit(solution)/shard_map/pallas_call | solution.py:196
  62.1 0.0 copy-done.3
  62.2 13.6 %shard_map.75.x_ref = bf16[2,4,512,128]{3,2,1,0:T(8,128)(2,1)S(1)} custom-call(s32[4096]{0:T(1024)S(1)} %bitcast.6, s32[1]{0:T(128)S(6)} %copy.8.count, bf16[2,256,16,128]{3,2,1,0:T(8,128)(2,1)S(1)} %bitcast.4), custom_call_target="tpu_custom_call" | custom-call | tf_op jit(solution)/shard_map/pallas_call | solution.py:111
  75.8 9.5 %shard_map.76.x_ref = bf16[2,4,512,128]{3,2,1,0:T(8,128)(2,1)S(1)} custom-call(bf16[2,4,512,128]{3,2,1,0:T(8,128)(2,1)S(1)} %shard_map.75.x_ref), custom_call_target="tpu_custom_call" | custom-call | tf_op jit(solution)/shard_map/pallas_call | solution.py:214
  85.2 0.0 copy-done.1
  85.3 4.3 %shard_map.77 = f32[512,2001]{1,0:T(8,128)} custom-call(bf16[2,4,512,128]{3,2,1,0:T(8,128)(2,1)S(1)} %shard_map.76.x_ref, bf16[1024,2001]{1,0:T(8,128)(2,1)S(1)} %copy-done.1), custom_call_target="tpu_custom_call" | custom-call | tf_op jit(solution)/shard_map/pallas_call | solution.py:126
Async XLA Ops:
  0.0 0.9 %copy-start = (s32[32,32,8]{1,2,0:T(8,128)S(1)}, s32[32,32,8]{1,2,0:T(8,128)}, u32[]{:S(2)}) copy-start(s32[32,32,8]{1,2,0:T(8,128)} %param.8) | copy-start | bytes 98308
  1.7 60.4 %copy-start.3 = (s32[16,2,128]{2,1,0:T(2,128)S(1)}, s32[16,2,128]{2,1,0:T(2,128)}, u32[]{:S(2)}) copy-start(s32[16,2,128]{2,1,0:T(2,128)} %param.9) | copy-start | bytes 49156
  17.2 68.0 %copy-start.1 = (bf16[1024,2001]{1,0:T(8,128)(2,1)S(1)}, bf16[1024,2001]{1,0:T(8,128)(2,1)}, u32[]{:S(2)}) copy-start(bf16[1024,2001]{1,0:T(8,128)(2,1)} %constant.18.clone.t_ref) | copy-start | bytes 12294148
  17.2 1.2 %copy-start.2 = (bf16[8,256,128]{2,1,0:T(8,128)(2,1)S(1)}, bf16[8,256,128]{2,1,0:T(8,128)(2,1)}, u32[]{:S(2)}) copy-start(bf16[8,256,128]{2,1,0:T(8,128)(2,1)} %shard_map.73) | copy-start | bytes 1572868

commit v2 on v0

v2 whole, which is shorter than its diff:
```python
import functools
import math

import jax
import jax.numpy as jnp
import ml_dtypes
import numpy as np
from jax import lax
from jax.experimental import pallas as pl
from jax.experimental.pallas import tpu as pltpu
from jax.sharding import PartitionSpec as P

MESH=pl.DeviceIdType.MESH
S=14976
def quarter_table():
    s=np.arange(3840)[:,None]; k=np.arange(512)[None]+60
    a=((s*k)%S)*(2*math.pi/S)
    c=np.cos(a).reshape(3840,8,1,64); d=-np.sin(a).reshape(3840,8,1,64)
    return np.concatenate([c,d],2).reshape(3840,1024).astype(ml_dtypes.bfloat16)
def turn_rows():
    lane=np.arange(1024)%128; k=(np.arange(1024)//128)*64+lane%64; im=lane>=64
    s=np.where(k%2==0,1.,-1.)
    al=np.array([1,0,-1,0.])[k%4]
    be=np.where(im,np.array([0,-1,0,1.])[k%4],np.array([0,1,0,-1.])[k%4])
    return np.stack([s,al,be]+[s*0]*5).astype(np.float32)
FIRST=(0,30,59,88); COUNT=(30,29,29,29); SHIFT=(0,96,64,32)
def lag_rows():
    k=np.arange(512)[:,None]+60; l=np.arange(2001)[None]-1000+S
    a=((k*l)%S)*(2*math.pi/S); s=1/math.sqrt(8192)
    t=np.stack([(np.cos(a)*s).reshape(8,64,2001),(-np.sin(a)*s).reshape(8,64,2001)],1)
    return t.reshape(1024,2001).astype(ml_dtypes.bfloat16)
def lag_kernel(x_ref,t_ref,o_ref):
    x=jnp.concatenate([x_ref[h,w] for h in range(2) for w in range(4)],1)
    o_ref[...]=jnp.dot(x,t_ref[...],preferred_element_type=jnp.float32)
def lag(x,tab):
    return pl.pallas_call(lag_kernel,out_shape=jax.ShapeDtypeStruct((512,2001),jnp.float32),grid=(4,),
      in_specs=[pl.BlockSpec((2,4,128,128),lambda i:(0,0,i,0)),pl.BlockSpec((1024,2001),lambda i:(0,0))],
      out_specs=pl.BlockSpec((128,2001),lambda i:(i,0)),
      compiler_params=pltpu.CompilerParams(vmem_limit_bytes=40<<20))(x,tab)


F=jnp.float32
B=jnp.bfloat16
HOPS=(0,2,1,3)

def whitened(acc,turn,h,b):
    cs=slice(512*h+128*b,512*h+128*b+128); gs=slice(128*b,128*b+128)
    s,al,be=turn[0:1,cs],turn[1:2,cs],turn[2:3,cs]
    g0,g1,g2,g3=(acc[q,:,gs] for q in range(4))
    z=g0+s*g2+al*(g1+g3)+be*pltpu.roll(g1-g3,64,1)
    sq=z*z
    mag=jnp.sqrt(sq+pltpu.roll(sq,64,1))
    level=jnp.sum(mag,axis=1,keepdims=True)*(1/128)+1e-6
    return (z*(1.0/level)).astype(B)

def whole(fr,slots,count,x_ref,t_ref,turn,o_ref,xs,ts,acc,wh,xr,xf,ff,dd,gg,ra,rb,tab,a1,a2,r1,r2,sr,part,
          xsem,tsem,sx,rx,s1,q1,s2,q2,sp,rp,ls):
    w=lax.axis_index("win"); me=lax.axis_index("chan")
    y,z,c=me//8,(me//2)%4,me%2
    dev=lambda yy,zz,cc:(w,yy*8+zz*2+cc)
    def send(src,dst,ss,rs,to):
        cp=pltpu.make_async_remote_copy(src_ref=src,dst_ref=dst,send_sem=ss,recv_sem=rs,device_id=to,device_id_type=MESH)
        cp.start()
        return cp
    def move(src,dst,sem):
        cp=pltpu.make_async_copy(src,dst,sem)
        cp.start()
        return cp
    tc=[pltpu.make_async_copy(t_ref.at[h],ts.at[h],tsem.at[h]) for h in range(2)]
    xc=[pltpu.make_async_copy(x_ref.at[:,:,pl.ds(128*FIRST[q],128*COUNT[q])],xs.at[:,:,pl.ds(128*FIRST[q],128*COUNT[q])],xsem.at[q]) for q in range(4)]
    tc[0].start()
    for q in range(4): xc[q].start()
    tc[1].start()
    bar=pltpu.get_barrier_semaphore()
    peers=[((w+d)%4,me) for d in (1,2,3)]+[dev((y+d)%4,z,(c+e)%2) for d in (1,2,3) for e in (0,1)]
    peers+=[dev(y,(z+d)%4,(c+e)%2) for d in range(4) for e in range(2) if (d,e)!=(0,0)]
    for p in peers: pl.semaphore_signal(bar,inc=1,device_id=p,device_id_type=MESH)

    def dft(h,q):
        if h==0: xc[q].wait()
        a,n=128*FIRST[q],128*COUNT[q]
        acc[q]=jnp.dot(xs[:,:,a:a+n].reshape(256,n),ts[h,SHIFT[q]:SHIFT[q]+n,:],preferred_element_type=F)
    def whiten(h):
        for b in range(4): wh[h,b]=whitened(acc,turn,h,b)
        cps=[send(wh.at[h,(w+d)%4],xr.at[h,w],sx.at[h,i],rx.at[h,i],((w+d)%4,me)) for i,d in enumerate((2,1,3))]
        return cps+[move(wh.at[h,w],xr.at[h,w],ls.at[h])]
    def pick(h,cps):
        for cp in cps: cp.wait()
        for s in range(4): xf[s]=xr[h,s].astype(F)
        for s in range(4):
            for i in range(4): ff[pl.ds(4*s+i,64,stride=16)]=xf[s,pl.ds(i,64,stride=4)]
        dd[h]=ff[...].astype(B).reshape(64,16,128)
        def owner(o,_):
            for j in range(8):
                gg[h,j//4,o//8,(o//2)%4,o%2,pl.ds(16*(j%4),16)]=dd[h,fr[o*8+j]]
            return 0
        lax.fori_loop(0,32,owner,0)
    def second(h,k):
        ys,zs=(y-HOPS[k])%4,(z-HOPS[k])%4
        cps=[]; j=0
        for dz in (2,1,3,0):
            for dc in (1,0):
                zz,yy,cc=(z+dz)%4,(y+dz)%4,(c+dc)%2
                if (dz,dc)==(0,0):
                    cps.append(move(ra.at[h,ys,z,c],tab.at[h,ys,z,c,0],ls.at[6+8*h+2*k]))
                    cps.append(move(rb.at[h,zs,y,c],tab.at[h,y,zs,c,1],ls.at[7+8*h+2*k]))
                    continue
                cps.append(send(ra.at[h,ys,zz,cc],tab.at[h,ys,z,c,0],s2.at[h,0,k,j],q2.at[h,0,k,j],dev(y,zz,cc)))
                cps.append(send(rb.at[h,zs,yy,cc],tab.at[h,y,zs,c,1],s2.at[h,1,k,j],q2.at[h,1,k,j],dev(yy,z,cc)))
                j+=1
        return cps
    def first(h):
        cps=[]
        for i,d in enumerate(HOPS[1:]):
            yy,zz=(y+d)%4,(z+d)%4
            cps.append((send(gg.at[h,0,yy],ra.at[h,y],s1.at[h,0,i],q1.at[h,0,i],dev(yy,z,c)),
                        send(gg.at[h,1,:,zz],rb.at[h,z],s1.at[h,1,i],q1.at[h,1,i],dev(y,zz,c))))
        own=[move(gg.at[h,0,y],ra.at[h,y],ls.at[2+2*h]),move(gg.at[h,1,:,z],rb.at[h,z],ls.at[3+2*h])]
        for cp in own: cp.wait()
        return cps,second(h,0)
    def forward(h,cps):
        out=[]
        for k in range(3):
            for cp in cps[k]: cp.wait()
            out+=second(h,k+1)
        return out
    ri=lax.broadcasted_iota(jnp.int32,(128,128),0); ci=lax.broadcasted_iota(jnp.int32,(128,128),1)
    lo=ci<64
    unit=lambda m,v: jnp.where(m,v,0.0).astype(B)
    turns=jnp.concatenate([unit(ri==ci+jnp.where(lo,64,-64),jnp.where(lo,1.0,-1.0)),unit(ri==ci-jnp.where(lo,0,64),1.0),unit(ri==ci+jnp.where(lo,64,0),1.0)],1)
    def spread(h):
        def block(i,_):
            v=tab[h,i//4,i%4].reshape(256,128)
            v2=jnp.dot(v,turns,preferred_element_type=F)
            rows=pl.ds(i*16,16)
            a1[h,rows]=v.astype(F).reshape(16,16,128)
            for m,ref in enumerate((a2,r1,r2)): ref[h,rows]=v2[:,128*m:128*m+128].reshape(16,16,128)
            return 0
        lax.fori_loop(0,16,block,0)
    live=count[0]
    def cross(h,t):
        keep=jnp.where(t<live,1.0,0.0).astype(F)
        def reduce(g):
            v=[sr[g,pl.ds(j,32,stride=8)] for j in range(8)]
            v=((v[0]+v[1])+(v[2]+v[3]))+((v[4]+v[5])+(v[6]+v[7]))
            part[h,g,pl.ds(pl.multiple_of(t*32,32),32)]=(v*keep).astype(B)
        for g in range(4):
            for i in range(32):
                s=slots[t*256+g*32+i]; r=slots[t*256+128+g*32+i]
                v=a1[h,s]*r1[h,r]+a2[h,s]*r2[h,r]
                sr[g,pl.ds(8*i,8)]=v[:8]+v[8:]
            if g: reduce(g-1)
        reduce(3)
    def hand_over(h,n):
        def tile(t,_):
            cross(h,4*n+t)
            return 0
        lax.fori_loop(0,4,tile,0)
        rows=pl.ds(128*n,128)
        cps=[send(part.at[h,(w+d)%4,rows],o_ref.at[h,w,rows],sp.at[h,n,i],rp.at[h,n,i],((w+d)%4,me)) for i,d in enumerate((2,1,3))]
        return cps+[move(part.at[h,w,rows],o_ref.at[h,w,rows],ls.at[22+4*h+n])]

    tc[0].wait()
    for q in range(4): dft(0,q)
    for b in range(4): wh[0,b]=whitened(acc,turn,0,b)
    pl.semaphore_wait(bar,len(peers))
    px0=[send(wh.at[0,(w+d)%4],xr.at[0,w],sx.at[0,i],rx.at[0,i],((w+d)%4,me)) for i,d in enumerate((2,1,3))]
    px0.append(move(wh.at[0,w],xr.at[0,w],ls.at[0]))
    tc[1].wait()
    for q in range(3): dft(1,q)
    pick(0,px0)
    p1a,p2a=first(0)
    dft(1,3)
    px1=whiten(1)
    p2a+=forward(0,p1a)
    pick(1,px1)
    p1b,p2b=first(1)
    for cp in p2a: cp.wait()
    spread(0)
    p2b+=forward(1,p1b)
    last=[]
    for n in range(4): last+=hand_over(0,n)
    for cp in p2b: cp.wait()
    spread(1)
    for n in range(4): last+=hand_over(1,n)
    for cp in last: cp.wait()

def correlate(fr,slots,count,x,table,turn):
    D=pltpu.SemaphoreType.DMA; V=pltpu.VMEM
    smem=pl.BlockSpec(memory_space=pltpu.SMEM); far=pl.BlockSpec(memory_space=pl.ANY); near=pl.BlockSpec(memory_space=pltpu.VMEM)
    return pl.pallas_call(whole,out_shape=jax.ShapeDtypeStruct((2,4,512,128),B),
      in_specs=[smem,smem,smem,far,far,near],out_specs=near,
      scratch_shapes=[V((64,4,S),B),V((2,3840,512),B),V((4,256,512),F),V((2,4,256,128),B),V((2,4,256,128),B),V((4,256,128),F),V((1024,128),F),V((2,64,16,128),B),
        V((2,2,4,4,2,64,128),B),V((2,4,4,2,64,128),B),V((2,4,4,2,64,128),B),V((2,4,4,2,2,64,128),B)]+[V((2,256,16,128),F)]*4+[V((4,256,128),F),V((2,4,512,128),B),
        D((4,)),D((2,)),D((2,3)),D((2,3)),D((2,2,3)),D((2,2,3)),D((2,2,4,7)),D((2,2,4,7)),D((2,4,3)),D((2,4,3)),D((30,))],
      compiler_params=pltpu.CompilerParams(collective_id=1,has_side_effects=True,vmem_limit_bytes=58<<20))(fr,slots,count,x,table,turn)

def body(traces,fetch_rows,pair_slots,tile_count):
    fr=lax.dynamic_index_in_dim(fetch_rows,lax.axis_index("chan"),1,keepdims=False).reshape(-1)
    table=quarter_table()
    table=jnp.asarray(np.stack([table[:,:512],table[:,512:]]))
    full=correlate(fr,pair_slots.reshape(-1),tile_count,traces,table,jnp.asarray(turn_rows()))
    return lag(full,jnp.asarray(lag_rows())).reshape(16,32,2001)

def solution(mesh):
    return jax.shard_map(body,mesh=mesh,in_specs=(P("chan","win",None),P(),P("chan",None,None),P("chan")),
      out_specs=P("chan","win",None),check_vma=False)
```

time: 546 us -> 74.7 us (0.14)
  waiting for transfers between devices: 212 us -> 0 us
  other arithmetic: 186 us -> 0 us
  local copies, waits for them, and re-layouts: 92.9 us -> 4.98 us
  Pallas kernels: 0 us -> 68.3 us
  matrix products: 33.1 us -> 0 us
  between operations: 13.5 us -> 0.71 us
  loops' own time: 7.25 us -> 0 us
    reduce_scatter x1 -> x0, waiting for transfers between devices: 136 us -> none  [body(): summed = lax.psum_scatter(cross_all, 'win', scatter_dimension=1, tiled=True)]
    another operation x2 -> x0, other arithmetic: 132 us -> none
    all_gather x1 -> x0, waiting for transfers between devices: 75.6 us -> none  [body(): every_row = lax.all_gather(whitened, 'chan', axis=0, tiled=True)]
    gather x20 -> x0, local copies, waits for them, and re-layouts: 69.2 us -> none  [the longest x9 27.3 us: cross_spectra(): jnp.take(channel_table, tile_slots[:, 1, :], axis=0).astype(jnp.float32)]
    pallas_call x0 -> x2, Pallas kernels: none -> 68.3 us  [the longest x1 64.1 us: correlate(): pl.pallas_call(whole, out_shape=jax.ShapeDtypeStruct((2, 4, 512, 128), B)...]
    dot_general x2 -> x0, matrix products: 33.1 us -> none  [the longest x1 17.7 us: body(): jnp.dot(summed.reshape(slot_count * share_width, 2 * FREQS), inverse, pre...]
    mul x2 -> x0, other arithmetic: 19.5 us -> none  [the longest x1 19.5 us: lag_table(): jnp.cos(angles) * lag_scale]
    reduce_sum x10 -> x0, other arithmetic: 14.3 us -> none  [the longest x9 14.1 us: cross_spectra(): jnp.sum(source_re * receiver_re + source_im * receiver_im, axis=2)]
  transfers between devices with their start and end apart: 2 -> 0, of which waited for: 2 -> 0; matrix products, arithmetic and copies ran while one was open for 4% -> 0% of each run, Pallas kernels for 0% -> 0%
where the time goes in v2:
time: 74.7 us; the launch traced here: 74 us
  Pallas kernels  68.3 us (91%)
  local copies, waits for them, and re-layouts  4.98 us (7%)
    pallas_call x1, Pallas kernels, correlate(): pl.pallas_call(whole, out_shape=jax.ShapeDtypeStruct((2, 4, 512, 128), B)...  64.1 us
    pallas_call x1, Pallas kernels, lag(): pl.pallas_call(lag_kernel, out_shape=jax.ShapeDtypeStruct((512, 2001), jn...  4.19 us
    unnamed x6, local copies, waits for them, and re-layouts  3.64 us

profile of v2, /device:TPU:1, one launch (start us, length us, event | category | flops | bytes accessed | tf_op | source)
XLA Modules:
  0.0 74.0 jit_solution(8158582291400347957)
XLA Ops:
  0.0 0.0 copy-start
  0.7 0.2 copy-done
  0.9 0.7 dynamic-slice_reduce_fusion
  1.6 0.7 reshape.10.fr
  2.3 64.1 %shard_map.73.x_ref = bf16[2,4,512,128]{3,2,1,0:T(8,128)(2,1)} custom-call(s32[256]{0:T(256)} %reshape.10.fr, s32[4096]{0:T(1024)} %bitcast.2, s32[1]{0:T(128)S(6)} %copy.8.count, bf16[64,4,14976]{2,1,0:T(4,128)(2,1)} %x_ref.1, bf16[2,3840,512]{2,1,0:T(8,128)(2,1)} %constant.16.clone.t_ref, f32[8,1024]{1,0:T(8,128)} %constant.17.clone.turn), custom_call_target="tpu_custom_call" | custom-call | tf_op jit(solution)/shard_map/pallas_call | solution.py:191
  66.4 0.0 copy-start.1
  66.4 1.2 %copy-done.1 = bf16[2,4,512,128]{3,2,1,0:T(8,128)(2,1)S(1)} copy-done((bf16[2,4,512,128]{3,2,1,0:T(8,128)(2,1)S(1)}, bf16[2,4,512,128]{3,2,1,0:T(8,128)(2,1)}, u32[]{:S(2)}) %copy-start.1) | copy-done | bytes 1048600
  67.6 0.0 copy-start.2
  67.6 2.2 %copy-done.2 = bf16[1024,2001]{1,0:T(8,128)(2,1)S(1)} copy-done((bf16[1024,2001]{1,0:T(8,128)(2,1)S(1)}, bf16[1024,2001]{1,0:T(8,128)(2,1)}, u32[]{:S(2)}) %copy-start.2) | copy-done | bytes 4098072
  69.8 4.2 %shard_map.74 = f32[512,2001]{1,0:T(8,128)} custom-call(bf16[2,4,512,128]{3,2,1,0:T(8,128)(2,1)S(1)} %copy-done.1, bf16[1024,2001]{1,0:T(8,128)(2,1)S(1)} %copy-done.2), custom_call_target="tpu_custom_call" | custom-call | tf_op jit(solution)/shard_map/pallas_call | solution.py:36
Async XLA Ops:
  0.0 0.9 %copy-start = (s32[32,32,8]{1,2,0:T(8,128)S(1)}, s32[32,32,8]{1,2,0:T(8,128)}, u32[]{:S(2)}) copy-start(s32[32,32,8]{1,2,0:T(8,128)} %param.8) | copy-start | bytes 98308
  66.4 1.2 %copy-start.1 = (bf16[2,4,512,128]{3,2,1,0:T(8,128)(2,1)S(1)}, bf16[2,4,512,128]{3,2,1,0:T(8,128)(2,1)}, u32[]{:S(2)}) copy-start(bf16[2,4,512,128]{3,2,1,0:T(8,128)(2,1)} %shard_map.73.x_ref) | copy-start | bytes 3145732
  67.6 2.2 %copy-start.2 = (bf16[1024,2001]{1,0:T(8,128)(2,1)S(1)}, bf16[1024,2001]{1,0:T(8,128)(2,1)}, u32[]{:S(2)}) copy-start(bf16[1024,2001]{1,0:T(8,128)(2,1)} %constant.18.clone.t_ref) | copy-start | bytes 12294148

commit v3 on v2

v3 whole, which is shorter than its diff:
```python
import functools
import math

import jax
import jax.numpy as jnp
import ml_dtypes
import numpy as np
from jax import lax
from jax.experimental import pallas as pl
from jax.experimental.pallas import tpu as pltpu
from jax.sharding import PartitionSpec as P

MESH=pl.DeviceIdType.MESH
S=14976
def quarter_table():
    s=np.arange(3840)[:,None]; k=np.arange(512)[None]+60
    a=((s*k)%S)*(2*math.pi/S)
    c=np.cos(a).reshape(3840,8,1,64); d=-np.sin(a).reshape(3840,8,1,64)
    return np.concatenate([c,d],2).reshape(3840,1024).astype(ml_dtypes.bfloat16)
FIRST=(0,30,59,88); COUNT=(30,29,29,29); SHIFT=(0,96,64,32)
def lag_rows():
    k=np.arange(512)[:,None]+60; l=np.arange(2001)[None]-1000+S
    a=((k*l)%S)*(2*math.pi/S); s=1/math.sqrt(8192)
    t=np.stack([(np.cos(a)*s).reshape(8,64,2001),(-np.sin(a)*s).reshape(8,64,2001)],1)
    return t.reshape(1024,2001).astype(ml_dtypes.bfloat16)
F=jnp.float32
B=jnp.bfloat16
HOPS=(0,2,1,3)

def lag_kernel(x_ref,t_ref,o_ref,buf,sem):
    cps=[]
    for i in range(4):
        rows=slice(128*i,128*i+128)
        x=jnp.concatenate([x_ref[h,w,rows] for h in range(2) for w in range(4)],1)
        buf[rows]=jnp.dot(x,t_ref[...],preferred_element_type=F)
        cp=pltpu.make_async_copy(buf.at[rows],o_ref.at[rows],sem.at[i])
        cp.start(); cps.append(cp)
    for cp in cps: cp.wait()
def lag(x,tab):
    near=pl.BlockSpec(memory_space=pltpu.VMEM)
    return pl.pallas_call(lag_kernel,out_shape=jax.ShapeDtypeStruct((512,2001),F),in_specs=[near,near],
      out_specs=pl.BlockSpec(memory_space=pl.ANY),scratch_shapes=[pltpu.VMEM((512,2001),F),pltpu.SemaphoreType.DMA((4,))],
      compiler_params=pltpu.CompilerParams(vmem_limit_bytes=20<<20))(x,tab)

def whole(lists,slots,count,x_ref,t_ref,o_ref,fr,xs,ts,acc,wh,xr,xf,ff,dd,gg,ra,rb,tab,a1,a2,r1,r2,sr,part,
          fsem,xsem,tsem,sx,rx,s1,q1,s2,q2,sp,rp,ls):
    w=lax.axis_index("win"); me=lax.axis_index("chan")
    y,z,c=me//8,(me//2)%4,me%2
    dev=lambda yy,zz,cc:(w,yy*8+zz*2+cc)
    def send(src,dst,ss,rs,to):
        cp=pltpu.make_async_remote_copy(src_ref=src,dst_ref=dst,send_sem=ss,recv_sem=rs,device_id=to,device_id_type=MESH)
        cp.start()
        return cp
    def move(src,dst,sem):
        cp=pltpu.make_async_copy(src,dst,sem)
        cp.start()
        return cp
    tc=[pltpu.make_async_copy(t_ref.at[h],ts.at[h],tsem.at[h]) for h in range(2)]
    xc=[pltpu.make_async_copy(x_ref.at[:,:,pl.ds(128*FIRST[q],128*COUNT[q])],xs.at[:,:,pl.ds(128*FIRST[q],128*COUNT[q])],xsem.at[q]) for q in range(4)]
    tc[0].start()
    for q in range(4): xc[q].start()
    fc=pltpu.make_async_copy(lists,fr,fsem)
    fc.start()
    tc[1].start()
    bar=pltpu.get_barrier_semaphore()
    peers=[((w+d)%4,me) for d in (1,2,3)]+[dev((y+d)%4,z,(c+e)%2) for d in (1,2,3) for e in (0,1)]
    peers+=[dev(y,(z+d)%4,(c+e)%2) for d in range(4) for e in range(2) if (d,e)!=(0,0)]
    for p in peers: pl.semaphore_signal(bar,inc=1,device_id=p,device_id_type=MESH)

    def dft(h,q):
        if h==0: xc[q].wait()
        a,n=128*FIRST[q],128*COUNT[q]
        acc[q]=jnp.dot(xs[:,:,a:a+n].reshape(256,n),ts[h,SHIFT[q]:SHIFT[q]+n,:],preferred_element_type=F)
    lane=lax.broadcasted_iota(jnp.int32,(1,128),1)
    four=lane%4
    sg=(1-2*(lane%2)).astype(F)
    al=jnp.where(four==0,1.0,jnp.where(four==2,-1.0,0.0)).astype(F)
    be=jnp.where(four==1,1.0,jnp.where(four==3,-1.0,0.0)).astype(F)*jnp.where(lane<64,1.0,-1.0).astype(F)
    def whiten(h):
        for b in range(4):
            g0,g1,g2,g3=(acc[q,:,128*b:128*b+128] for q in range(4))
            v=g0+sg*g2+al*(g1+g3)+be*pltpu.roll(g1-g3,64,1)
            sq=v*v
            sq=sq+pltpu.roll(sq,64,1)
            mag=sq*lax.rsqrt(jnp.maximum(sq,1e-30))
            level=jnp.sum(mag,axis=1,keepdims=True)*(1/128)+1e-6
            wh[h,b]=(v*(1.0/level)).astype(B)
    def spectra(h):
        return [send(wh.at[h,(w+d)%4],xr.at[h,w],sx.at[h,i],rx.at[h,i],((w+d)%4,me)) for i,d in enumerate((2,1,3))]
    def pick(h,cps):
        for cp in cps: cp.wait()
        for d in range(4):
            xf[d]=(xr if d else wh)[h,(w+d)%4].astype(F)
        for d in range(4):
            for i in range(4): ff[pl.ds(4*d+i,64,stride=16)]=xf[d,pl.ds(i,64,stride=4)]
        dd[h]=ff[...].astype(B).reshape(64,16,128)
        def owner(o,_):
            for j in range(8):
                gg[h,j//4,o//8,(o//2)%4,o%2,pl.ds(16*(j%4),16)]=dd[h,fr[o,j,me]]
            return 0
        lax.fori_loop(0,32,owner,0)
    def second(h,k):
        ys,zs=(y-HOPS[k])%4,(z-HOPS[k])%4
        cps=[]; j=0
        for dz in (2,1,3,0):
            for dc in (1,0):
                zz,yy,cc=(z+dz)%4,(y+dz)%4,(c+dc)%2
                fa=ra.at[h,ys,zz,cc] if k else gg.at[h,0,y,zz,cc]
                fb=rb.at[h,zs,yy,cc] if k else gg.at[h,1,yy,z,cc]
                if (dz,dc)==(0,0):
                    cps.append(move(fa,tab.at[h,ys,z,c,0],ls.at[6+8*h+2*k]))
                    cps.append(move(fb,tab.at[h,y,zs,c,1],ls.at[7+8*h+2*k]))
                    continue
                cps.append(send(fa,tab.at[h,ys,z,c,0],s2.at[h,0,k,j],q2.at[h,0,k,j],dev(y,zz,cc)))
                cps.append(send(fb,tab.at[h,y,zs,c,1],s2.at[h,1,k,j],q2.at[h,1,k,j],dev(yy,z,cc)))
                j+=1
        return cps
    def first(h):
        cps=[]
        for i,d in enumerate(HOPS[1:]):
            yy,zz=(y+d)%4,(z+d)%4
            cps.append((send(gg.at[h,0,yy],ra.at[h,y],s1.at[h,0,i],q1.at[h,0,i],dev(yy,z,c)),
                        send(gg.at[h,1,:,zz],rb.at[h,z],s1.at[h,1,i],q1.at[h,1,i],dev(y,zz,c))))
        return cps,second(h,0)
    def forward(h,cps):
        out=[]
        for k in range(3):
            for cp in cps[k]: cp.wait()
            out+=second(h,k+1)
        return out
    ri=lax.broadcasted_iota(jnp.int32,(128,128),0); ci=lax.broadcasted_iota(jnp.int32,(128,128),1)
    lo=ci<64
    unit=lambda m,v: jnp.where(m,v,0.0).astype(B)
    turns=jnp.concatenate([unit(ri==ci+jnp.where(lo,64,-64),jnp.where(lo,1.0,-1.0)),unit(ri==ci-jnp.where(lo,0,64),1.0),unit(ri==ci+jnp.where(lo,64,0),1.0)],1)
    def spread(h):
        def block(i,_):
            v=tab[h,i//4,i%4].reshape(256,128)
            v2=jnp.dot(v,turns,preferred_element_type=F)
            rows=pl.ds(i*16,16)
            a1[h,rows]=v.astype(F).reshape(16,16,128)
            for m,ref in enumerate((a2,r1,r2)): ref[h,rows]=v2[:,128*m:128*m+128].reshape(16,16,128)
            return 0
        lax.fori_loop(0,16,block,0)
    live=count[0]
    def cross(h,t):
        keep=jnp.where(t<live,1.0,0.0).astype(F)
        def reduce(g):
            v=[sr[g,pl.ds(j,32,stride=8)] for j in range(8)]
            v=((v[0]+v[1])+(v[2]+v[3]))+((v[4]+v[5])+(v[6]+v[7]))
            part[h,g,pl.ds(pl.multiple_of(t*32,32),32)]=(v*keep).astype(B)
        for g in range(4):
            for i in range(32):
                s=slots[t*256+g*32+i]; r=slots[t*256+128+g*32+i]
                v=a1[h,s]*r1[h,r]+a2[h,s]*r2[h,r]
                sr[g,pl.ds(8*i,8)]=v[:8]+v[8:]
            if g: reduce(g-1)
        reduce(3)
    def hand_over(h,n):
        def tile(t,_):
            cross(h,4*n+t)
            return 0
        lax.fori_loop(0,4,tile,0)
        rows=pl.ds(128*n,128)
        cps=[send(part.at[h,(w+d)%4,rows],o_ref.at[h,w,rows],sp.at[h,n,i],rp.at[h,n,i],((w+d)%4,me)) for i,d in enumerate((2,1,3))]
        return cps+[move(part.at[h,w,rows],o_ref.at[h,w,rows],ls.at[22+4*h+n])]

    tc[0].wait()
    for q in range(4): dft(0,q)
    whiten(0)
    pl.semaphore_wait(bar,len(peers))
    px0=spectra(0)
    tc[1].wait()
    for q in range(3): dft(1,q)
    fc.wait()
    pick(0,px0)
    p1a,p2a=first(0)
    dft(1,3)
    whiten(1)
    px1=spectra(1)
    p2a+=forward(0,p1a)
    pick(1,px1)
    p1b,p2b=first(1)
    for cp in p2a: cp.wait()
    spread(0)
    last=hand_over(0,0)
    p2b+=forward(1,p1b)
    for n in range(1,4): last+=hand_over(0,n)
    for cp in p2b: cp.wait()
    spread(1)
    for n in range(4): last+=hand_over(1,n)
    for cp in last: cp.wait()

def correlate(lists,slots,count,x,table):
    D=pltpu.SemaphoreType.DMA; V=pltpu.VMEM
    smem=pl.BlockSpec(memory_space=pltpu.SMEM); far=pl.BlockSpec(memory_space=pl.ANY); near=pl.BlockSpec(memory_space=pltpu.VMEM)
    return pl.pallas_call(whole,out_shape=jax.ShapeDtypeStruct((2,4,512,128),B),
      in_specs=[far,smem,smem,far,far],out_specs=near,
      scratch_shapes=[pltpu.SMEM((32,8,32),jnp.int32),V((64,4,S),B),V((2,3840,512),B),V((4,256,512),F),V((2,4,256,128),B),V((2,4,256,128),B),V((4,256,128),F),V((1024,128),F),V((2,64,16,128),B),
        V((2,2,4,4,2,64,128),B),V((2,4,4,2,64,128),B),V((2,4,4,2,64,128),B),V((2,4,4,2,2,64,128),B)]+[V((2,256,16,128),F)]*4+[V((4,256,128),F),V((2,4,512,128),B),
        D,D((4,)),D((2,)),D((2,3)),D((2,3)),D((2,2,3)),D((2,2,3)),D((2,2,4,7)),D((2,2,4,7)),D((2,4,3)),D((2,4,3)),D((30,))],
      compiler_params=pltpu.CompilerParams(collective_id=1,has_side_effects=True,vmem_limit_bytes=50<<20))(lists,slots,count,x,table)

def body(traces,fetch_rows,pair_slots,tile_count):
    table=quarter_table()
    table=jnp.asarray(np.stack([table[:,:512],table[:,512:]]))
    full=correlate(fetch_rows.transpose(0,2,1),pair_slots.reshape(-1),tile_count,traces,table)
    return lag(full,jnp.asarray(lag_rows())).reshape(16,32,2001)

def solution(mesh):
    return jax.shard_map(body,mesh=mesh,in_specs=(P("chan","win",None),P(),P("chan",None,None),P("chan")),
      out_specs=P("chan","win",None),check_vma=False)
```

time: 74.7 us -> 70.1 us (0.938)
  local copies, waits for them, and re-layouts: 4.98 us -> 1.62 us
  Pallas kernels: 68.3 us -> 67 us
    unnamed x6, local copies, waits for them, and re-layouts: 3.64 us -> 1.62 us
    pallas_call x1, Pallas kernels: 4.19 us -> 3.37 us  [lag(): pl.pallas_call(lag_kernel, out_shape=jax.ShapeDtypeStruct((512, 2001), F)...]
where the time goes in v3:
time: 70.1 us; the launch traced here: 69.5 us
  Pallas kernels  67 us (96%)
  local copies, waits for them, and re-layouts  1.62 us (2%)
  between operations  0.84 us (1%)
    pallas_call x1, Pallas kernels, correlate(): pl.pallas_call(whole, out_shape=jax.ShapeDtypeStruct((2, 4, 512, 128), B)...  63.7 us
    pallas_call x1, Pallas kernels, lag(): pl.pallas_call(lag_kernel, out_shape=jax.ShapeDtypeStruct((512, 2001), F)...  3.37 us
    unnamed x6, local copies, waits for them, and re-layouts  1.62 us

profile of v3, /device:TPU:1, one launch (start us, length us, event | category | flops | bytes accessed | tf_op | source)
XLA Modules:
  0.0 69.5 jit_solution(14255434905072242170)
XLA Ops:
  0.7 0.0 copy-start.1
  0.7 0.9 %copy-done.1 = s32[32,32,8]{1,2,0:T(8,128)S(1)} copy-done((s32[32,32,8]{1,2,0:T(8,128)S(1)}, s32[32,32,8]{1,2,0:T(8,128)}, u32[]{:S(2)}) %copy-start.1) | copy-done | bytes 32792
  1.6 0.0 copy-start.2
  1.6 0.7 %copy-done.2 = s32[16,2,128]{2,1,0:T(2,128)S(1)} copy-done((s32[16,2,128]{2,1,0:T(2,128)S(1)}, s32[16,2,128]{2,1,0:T(2,128)}, u32[]{:S(2)}) %copy-start.2) | copy-done | bytes 16408
  2.3 0.0 copy-start
  2.3 63.7 %shard_map.64.x_ref = bf16[2,4,512,128]{3,2,1,0:T(8,128)(2,1)S(1)} custom-call(s32[32,8,32]{2,1,0:T(8,128)S(1)} %bitcast.3, s32[4096]{0:T(1024)S(1)} %bitcast.4, s32[1]{0:T(128)S(6)} %copy.7.count, bf16[64,4,14976]{2,1,0:T(4,128)(2,1)} %x_ref.1, bf16[2,3840,512]{2,1,0:T(8,128)(2,1)} %constant.4.clone.t_ref), custom_call_target="tpu_custom_call" | custom-call | tf_op jit(solution)/shard_map/pallas_call | solution.py:196
  65.9 0.0 copy-done
  66.0 3.4 %shard_map.65 = f32[512,2001]{1,0:T(8,128)} custom-call(bf16[2,4,512,128]{3,2,1,0:T(8,128)(2,1)S(1)} %shard_map.64.x_ref, bf16[1024,2001]{1,0:T(8,128)(2,1)S(1)} %copy-done), custom_call_target="tpu_custom_call" | custom-call | tf_op jit(solution)/shard_map/pallas_call | solution.py:41
Async XLA Ops:
  0.7 0.9 %copy-start.1 = (s32[32,32,8]{1,2,0:T(8,128)S(1)}, s32[32,32,8]{1,2,0:T(8,128)}, u32[]{:S(2)}) copy-start(s32[32,32,8]{1,2,0:T(8,128)} %param.7) | copy-start | bytes 98308
  1.6 0.7 %copy-start.2 = (s32[16,2,128]{2,1,0:T(2,128)S(1)}, s32[16,2,128]{2,1,0:T(2,128)}, u32[]{:S(2)}) copy-start(s32[16,2,128]{2,1,0:T(2,128)} %param.8) | copy-start | bytes 49156
  2.3 63.7 %copy-start = (bf16[1024,2001]{1,0:T(8,128)(2,1)S(1)}, bf16[1024,2001]{1,0:T(8,128)(2,1)}, u32[]{:S(2)}) copy-start(bf16[1024,2001]{1,0:T(8,128)(2,1)} %constant.5.clone.t_ref) | copy-start | bytes 12294148

commit v4 on v3

--- a/solution.py
+++ b/solution.py
@@ -26,6 +26,7 @@
 F=jnp.float32
 B=jnp.bfloat16
 HOPS=(0,2,1,3)
+GROUPS=((0,4,8,12,16),(0,2,6,11,16))
 
 def lag_kernel(x_ref,t_ref,o_ref,buf,sem):
     cps=[]
@@ -122,9 +123,9 @@
             cps.append((send(gg.at[h,0,yy],ra.at[h,y],s1.at[h,0,i],q1.at[h,0,i],dev(yy,z,c)),
                         send(gg.at[h,1,:,zz],rb.at[h,z],s1.at[h,1,i],q1.at[h,1,i],dev(y,zz,c))))
         return cps,second(h,0)
-    def forward(h,cps):
+    def forward(h,cps,hops=range(3)):
         out=[]
-        for k in range(3):
+        for k in hops:
             for cp in cps[k]: cp.wait()
             out+=second(h,k+1)
         return out
@@ -132,15 +133,21 @@
     lo=ci<64
     unit=lambda m,v: jnp.where(m,v,0.0).astype(B)
     turns=jnp.concatenate([unit(ri==ci+jnp.where(lo,64,-64),jnp.where(lo,1.0,-1.0)),unit(ri==ci-jnp.where(lo,0,64),1.0),unit(ri==ci+jnp.where(lo,64,0),1.0)],1)
-    def spread(h):
-        def block(i,_):
-            v=tab[h,i//4,i%4].reshape(256,128)
-            v2=jnp.dot(v,turns,preferred_element_type=F)
-            rows=pl.ds(i*16,16)
-            a1[h,rows]=v.astype(F).reshape(16,16,128)
-            for m,ref in enumerate((a2,r1,r2)): ref[h,rows]=v2[:,128*m:128*m+128].reshape(16,16,128)
-            return 0
-        lax.fori_loop(0,16,block,0)
+    def spread(h,cps):
+        for k in range(4):
+            for cp in cps[16*k:16*k+16]: cp.wait()
+            ys,zs=(y-HOPS[k])%4,(z-HOPS[k])%4
+            def block(i,_):
+                for r in range(2):
+                    yy,zz=(ys,i) if r==0 else (i,zs)
+                    v=tab[h,yy,zz,:,r].reshape(128,128)
+                    v2=jnp.dot(v,turns,preferred_element_type=F)
+                    parts=[v.astype(F)]+[v2[:,128*m:128*m+128] for m in range(3)]
+                    for cc in range(2):
+                        rows=pl.ds((yy*4+zz)*16+8*cc+4*r,4)
+                        for ref,u in zip((a1,a2,r1,r2),parts): ref[h,rows]=u[64*cc:64*cc+64].reshape(4,16,128)
+                return 0
+            lax.fori_loop(0,4,block,0)
     live=count[0]
     def cross(h,t):
         keep=jnp.where(t<live,1.0,0.0).astype(F)
@@ -156,11 +163,12 @@
             if g: reduce(g-1)
         reduce(3)
     def hand_over(h,n):
+        t0,t1=GROUPS[h][n:n+2]
         def tile(t,_):
-            cross(h,4*n+t)
+            cross(h,t)
             return 0
-        lax.fori_loop(0,4,tile,0)
-        rows=pl.ds(128*n,128)
+        lax.fori_loop(t0,t1,tile,0)
+        rows=pl.ds(32*t0,32*(t1-t0))
         cps=[send(part.at[h,(w+d)%4,rows],o_ref.at[h,w,rows],sp.at[h,n,i],rp.at[h,n,i],((w+d)%4,me)) for i,d in enumerate((2,1,3))]
         return cps+[move(part.at[h,w,rows],o_ref.at[h,w,rows],ls.at[22+4*h+n])]
 
@@ -180,13 +188,13 @@
     p2a+=forward(0,p1a)
     pick(1,px1)
     p1b,p2b=first(1)
-    for cp in p2a: cp.wait()
-    spread(0)
+    spread(0,p2a)
     last=hand_over(0,0)
-    p2b+=forward(1,p1b)
-    for n in range(1,4): last+=hand_over(0,n)
-    for cp in p2b: cp.wait()
-    spread(1)
+    p2b+=forward(1,p1b,(0,))
+    last+=hand_over(0,1)
+    p2b+=forward(1,p1b,(1,2))
+    for n in range(2,4): last+=hand_over(0,n)
+    spread(1,p2b)
     for n in range(4): last+=hand_over(1,n)
     for cp in last: cp.wait()
 

time: 70.1 us -> 67.9 us (0.969)
  Pallas kernels: 67 us -> 64.8 us
    pallas_call x1, Pallas kernels: 63.7 us -> 61.4 us  [correlate(): pl.pallas_call(whole, out_shape=jax.ShapeDtypeStruct((2, 4, 512, 128), B)...]
where the time goes in v4:
time: 67.9 us; the launch traced here: 67.2 us
  Pallas kernels  64.8 us (95%)
  local copies, waits for them, and re-layouts  1.62 us (2%)
  between operations  0.84 us (1%)
    pallas_call x1, Pallas kernels, correlate(): pl.pallas_call(whole, out_shape=jax.ShapeDtypeStruct((2, 4, 512, 128), B)...  61.4 us
    pallas_call x1, Pallas kernels, lag(): pl.pallas_call(lag_kernel, out_shape=jax.ShapeDtypeStruct((512, 2001), F)...  3.37 us
    unnamed x6, local copies, waits for them, and re-layouts  1.62 us

profile of v4, /device:TPU:1, one launch (start us, length us, event | category | flops | bytes accessed | tf_op | source)
XLA Modules:
  0.0 67.2 jit_solution(1528007522348493667)
XLA Ops:
  0.7 0.0 copy-start.1
  0.7 0.9 %copy-done.1 = s32[32,32,8]{1,2,0:T(8,128)S(1)} copy-done((s32[32,32,8]{1,2,0:T(8,128)S(1)}, s32[32,32,8]{1,2,0:T(8,128)}, u32[]{:S(2)}) %copy-start.1) | copy-done | bytes 32792
  1.6 0.0 copy-start.2
  1.6 0.7 %copy-done.2 = s32[16,2,128]{2,1,0:T(2,128)S(1)} copy-done((s32[16,2,128]{2,1,0:T(2,128)S(1)}, s32[16,2,128]{2,1,0:T(2,128)}, u32[]{:S(2)}) %copy-start.2) | copy-done | bytes 16408
  2.3 0.0 copy-start
  2.3 61.4 %shard_map.64.x_ref = bf16[2,4,512,128]{3,2,1,0:T(8,128)(2,1)S(1)} custom-call(s32[32,8,32]{2,1,0:T(8,128)S(1)} %bitcast.3, s32[4096]{0:T(1024)S(1)} %bitcast.4, s32[1]{0:T(128)S(6)} %copy.7.count, bf16[64,4,14976]{2,1,0:T(4,128)(2,1)} %x_ref.1, bf16[2,3840,512]{2,1,0:T(8,128)(2,1)} %constant.4.clone.t_ref), custom_call_target="tpu_custom_call" | custom-call | tf_op jit(solution)/shard_map/pallas_call | solution.py:204
  63.7 0.0 copy-done
  63.7 3.4 %shard_map.65 = f32[512,2001]{1,0:T(8,128)} custom-call(bf16[2,4,512,128]{3,2,1,0:T(8,128)(2,1)S(1)} %shard_map.64.x_ref, bf16[1024,2001]{1,0:T(8,128)(2,1)S(1)} %copy-done), custom_call_target="tpu_custom_call" | custom-call | tf_op jit(solution)/shard_map/pallas_call | solution.py:42
Async XLA Ops:
  0.7 0.9 %copy-start.1 = (s32[32,32,8]{1,2,0:T(8,128)S(1)}, s32[32,32,8]{1,2,0:T(8,128)}, u32[]{:S(2)}) copy-start(s32[32,32,8]{1,2,0:T(8,128)} %param.7) | copy-start | bytes 98308
  1.6 0.7 %copy-start.2 = (s32[16,2,128]{2,1,0:T(2,128)S(1)}, s32[16,2,128]{2,1,0:T(2,128)}, u32[]{:S(2)}) copy-start(s32[16,2,128]{2,1,0:T(2,128)} %param.8) | copy-start | bytes 49156
  2.3 61.4 %copy-start = (bf16[1024,2001]{1,0:T(8,128)(2,1)S(1)}, bf16[1024,2001]{1,0:T(8,128)(2,1)}, u32[]{:S(2)}) copy-start(bf16[1024,2001]{1,0:T(8,128)(2,1)} %constant.5.clone.t_ref) | copy-start | bytes 12294148

commit v5 on v4

--- a/solution.py
+++ b/solution.py
@@ -178,11 +178,10 @@
     pl.semaphore_wait(bar,len(peers))
     px0=spectra(0)
     tc[1].wait()
-    for q in range(3): dft(1,q)
+    for q in range(4): dft(1,q)
     fc.wait()
     pick(0,px0)
     p1a,p2a=first(0)
-    dft(1,3)
     whiten(1)
     px1=spectra(1)
     p2a+=forward(0,p1a)

time: 67.9 us -> 67.9 us (level)
  no operation moved by 1% of the time
where the time goes in v5:
time: 67.9 us; the launch traced here: 67.2 us
  Pallas kernels  64.8 us (95%)
  local copies, waits for them, and re-layouts  1.62 us (2%)
  between operations  0.84 us (1%)
    pallas_call x1, Pallas kernels, correlate(): pl.pallas_call(whole, out_shape=jax.ShapeDtypeStruct((2, 4, 512, 128), B)...  61.4 us
    pallas_call x1, Pallas kernels, lag(): pl.pallas_call(lag_kernel, out_shape=jax.ShapeDtypeStruct((512, 2001), F)...  3.38 us
    unnamed x6, local copies, waits for them, and re-layouts  1.62 us

profile of v5, /device:TPU:1, one launch (start us, length us, event | category | flops | bytes accessed | tf_op | source)
XLA Modules:
  0.0 67.2 jit_solution(8500356378186054168)
XLA Ops:
  0.7 0.0 copy-start.1
  0.7 0.9 %copy-done.1 = s32[32,32,8]{1,2,0:T(8,128)S(1)} copy-done((s32[32,32,8]{1,2,0:T(8,128)S(1)}, s32[32,32,8]{1,2,0:T(8,128)}, u32[]{:S(2)}) %copy-start.1) | copy-done | bytes 32792
  1.6 0.0 copy-start.2
  1.6 0.7 %copy-done.2 = s32[16,2,128]{2,1,0:T(2,128)S(1)} copy-done((s32[16,2,128]{2,1,0:T(2,128)S(1)}, s32[16,2,128]{2,1,0:T(2,128)}, u32[]{:S(2)}) %copy-start.2) | copy-done | bytes 16408
  2.3 0.0 copy-start
  2.3 61.4 %shard_map.64.x_ref = bf16[2,4,512,128]{3,2,1,0:T(8,128)(2,1)S(1)} custom-call(s32[32,8,32]{2,1,0:T(8,128)S(1)} %bitcast.3, s32[4096]{0:T(1024)S(1)} %bitcast.4, s32[1]{0:T(128)S(6)} %copy.7.count, bf16[64,4,14976]{2,1,0:T(4,128)(2,1)} %x_ref.1, bf16[2,3840,512]{2,1,0:T(8,128)(2,1)} %constant.4.clone.t_ref), custom_call_target="tpu_custom_call" | custom-call | tf_op jit(solution)/shard_map/pallas_call | solution.py:203
  63.7 0.0 copy-done
  63.7 3.4 %shard_map.65 = f32[512,2001]{1,0:T(8,128)} custom-call(bf16[2,4,512,128]{3,2,1,0:T(8,128)(2,1)S(1)} %shard_map.64.x_ref, bf16[1024,2001]{1,0:T(8,128)(2,1)S(1)} %copy-done), custom_call_target="tpu_custom_call" | custom-call | tf_op jit(solution)/shard_map/pallas_call | solution.py:42
Async XLA Ops:
  0.7 0.9 %copy-start.1 = (s32[32,32,8]{1,2,0:T(8,128)S(1)}, s32[32,32,8]{1,2,0:T(8,128)}, u32[]{:S(2)}) copy-start(s32[32,32,8]{1,2,0:T(8,128)} %param.7) | copy-start | bytes 98308
  1.6 0.7 %copy-start.2 = (s32[16,2,128]{2,1,0:T(2,128)S(1)}, s32[16,2,128]{2,1,0:T(2,128)}, u32[]{:S(2)}) copy-start(s32[16,2,128]{2,1,0:T(2,128)} %param.8) | copy-start | bytes 49156
  2.3 61.4 %copy-start = (bf16[1024,2001]{1,0:T(8,128)(2,1)S(1)}, bf16[1024,2001]{1,0:T(8,128)(2,1)}, u32[]{:S(2)}) copy-start(bf16[1024,2001]{1,0:T(8,128)(2,1)} %constant.5.clone.t_ref) | copy-start | bytes 12294148
